TPU v7x, 512 devices: a whole 4x4x16 slice. The times are simulated.
512 devices in a mesh: hst: 64 (over y, z_lo, core), head: 8 (over x, z_hi).
Axes of the slice: x: 4, y: 4, z: 16 (z_hi: 2, z_lo: 8; z = z_hi * 8 + z_lo), core: 2. Of those that a mesh axis runs over, the one named last changes fastest.
Arguments:
- queries: bfloat16 [16384, 4096], P('hst', 'head')
- keys: bfloat16 [16384, 1024], P('hst', 'head')
- values: bfloat16 [16384, 1024], P('hst', 'head'), may hold values from -24 to 24
- passing_index: int32 [64, 128], P('hst'), may hold values from 0 to 255, as said below
- out_weight: bfloat16 [4096, 4096], P('head'), may hold values from -0.09375 to 0.09375
Outputs:
- mixed: bfloat16 [16384, 4096], P('hst', 'head')
Inputs may be any that keep to these rules, and one draw needn't show every extreme that they name: `passing_index`: each shard's 128 positions are distinct.
All inputs are finite; a program needn't handle non-finite values.
Results may differ from a plain program's by a relative error of at most 0.019.
Values may be sent and summed in bfloat16 or wider, within the bound.
No kernel may reach another device: no remote copies, remote signals or barrier semaphores. Data moves between devices by JAX's collectives and lax.ppermute only.
A program may use at most 64 MiB of HBM per device.

v0:
```python
import math

import jax
import jax.numpy as jnp
from jax import lax
from jax.sharding import PartitionSpec as P

QH = 32
KVH = 8
HD = 128
PASS = 128
ANCHOR = 128


neg_big = -1e30


def from_root(value, axis, root):
    mine = lax.axis_index(axis) == root
    return lax.psum(jnp.where(mine, value, jnp.zeros_like(value)), axis)


def online_step(carried, query_heads, key_block, value_block, visible):
    weighted, running_max, row_mass = carried
    key_count = key_block.shape[0]
    kv_local = query_heads.shape[1]
    head_width = query_heads.shape[3]
    key_heads = key_block.reshape(key_count, kv_local, head_width)
    value_heads = value_block.reshape(key_count, kv_local, head_width)
    scores = jnp.einsum(
        "rkgd,nkd->kgrn", query_heads, key_heads, preferred_element_type=jnp.float32
    ) / math.sqrt(head_width)
    masked = jnp.where(visible, scores, neg_big)
    new_max = jnp.maximum(running_max, jnp.max(masked, axis=-1))
    shrink = jnp.exp(running_max - new_max)
    weights = jnp.where(visible, jnp.exp(masked - new_max[..., None]), 0.0)
    row_mass = row_mass * shrink + jnp.sum(weights, axis=-1)
    weighted = weighted * shrink[..., None] + jnp.einsum(
        "kgrn,nkd->kgrd",
        weights.astype(jnp.bfloat16),
        value_heads,
        preferred_element_type=jnp.float32,
    )
    return (weighted, new_max, row_mass)


def empty_state(kv_local, groups, row_count):
    return (
        jnp.zeros((kv_local, groups, row_count, HD), jnp.float32),
        jnp.full((kv_local, groups, row_count), neg_big, jnp.float32),
        jnp.zeros((kv_local, groups, row_count), jnp.float32),
    )


def passing_over(carried, query_heads, below_shard, piece_keys, piece_values):
    key_count = piece_keys.shape[0]
    sub_rows = PASS

    def visit_block(sub_index, state):
        first_key = sub_index * sub_rows
        key_part = lax.dynamic_slice_in_dim(piece_keys, sub_index * sub_rows, sub_rows, 0)
        value_part = lax.dynamic_slice_in_dim(piece_values, sub_index * sub_rows, sub_rows, 0)
        visible = ((first_key + jnp.arange(sub_rows)) // PASS < below_shard)[None, :]
        return lax.cond(
            first_key < below_shard * PASS,
            lambda inner: online_step(inner, query_heads, key_part, value_part, visible),
            lambda inner: inner,
            state,
        )

    return lax.fori_loop(0, key_count // sub_rows, visit_block, carried)


def shards(queries, keys, values, passing_index, out_weight):
    row_count = queries.shape[0]
    kv_local = keys.shape[1] // HD
    groups = QH // KVH
    shard_index = lax.axis_index("hst")
    query_heads = queries.reshape(row_count, kv_local, groups, HD)
    positions = jnp.arange(row_count)
    state = empty_state(kv_local, groups, row_count)
    state = online_step(state, query_heads, keys, values, positions[:, None] >= positions[None, :])
    anchor_keys, anchor_values = (
        from_root(keys[:ANCHOR], "hst", 0),
        from_root(values[:ANCHOR], "hst", 0),
    )
    state = online_step(
        state, query_heads, anchor_keys, anchor_values, jnp.full((1, ANCHOR), shard_index > 0)
    )
    chosen = passing_index[0]
    pass_keys = jnp.take(keys, chosen, axis=0)
    pass_values = jnp.take(values, chosen, axis=0)
    state = passing_over(
        state,
        query_heads,
        shard_index,
        lax.all_gather(pass_keys, "hst", axis=0, tiled=True),
        lax.all_gather(pass_values, "hst", axis=0, tiled=True),
    )
    weighted, running_max, row_mass = state
    attended = (
        (weighted / row_mass[..., None])
        .transpose(2, 0, 1, 3)
        .reshape(row_count, kv_local * groups * HD)
        .astype(jnp.bfloat16)
    )
    partial_sums = jnp.dot(attended, out_weight, preferred_element_type=jnp.float32)
    return lax.psum_scatter(
        partial_sums.astype(jnp.bfloat16), "head", scatter_dimension=1, tiled=True
    )


def solution(mesh):
    in_specs = (
        P("hst", "head"),
        P("hst", "head"),
        P("hst", "head"),
        P("hst", None),
        P("head", None),
    )
    out_specs = P("hst", "head")
    return jax.shard_map(shards, mesh=mesh, in_specs=in_specs, out_specs=out_specs, check_vma=False)
```

profile of v0, /device:TPU:6, one launch (start us, length us, event | category | flops | bytes accessed | tf_op | source)
XLA Modules:
  0.0 1320.6 jit_solution(8819492299042729058)
XLA Ops:
  6.5 0.0 copy-start.1
  6.5 0.0 copy-start
  6.5 0.0 all-reduce.3.cloned.1.call-start
  6.5 1.4 slice_select_fusion
  8.0 0.0 all-reduce.3.cloned.1.call-update
  8.0 0.0 all-gather.3.cloned.1.call-start
  8.1 0.7 compare_select_fusion.3
  8.7 1.5 gather_fusion
  10.2 1.5 gather_fusion.1
  11.7 0.0 copy-start.2
  11.7 0.7 compare_and_fusion
  12.4 0.7 broadcast_select_fusion
  13.1 0.0 all-gather.3.cloned.1.call-update
  13.2 0.0 all-gather.5.cloned.1.call-start
  13.2 0.7 all-gather.5.cloned.1.call-update
  13.9 0.0 reduce-scatter.2.cloned.1.call-start
  14.0 1.1 copy.16
  15.0 0.2 copy.17
  15.3 0.0 copy-done.1
  15.3 0.0 copy-done
  15.3 0.3 fusion.57
  15.6 753.6 %all-reduce.3.cloned.1.call-done = (bf16[128,128]{1,0:T(8,128)(2,1)}, bf16[128,128]{1,0:T(8,128)(2,1)}) async-done(((bf16[128,128]{1,0:T(8,128)(2,1)}, bf16[128,128]{1,0:T(8,128)(2,1)}), (bf16[128,128]{1,0:T(8,128)(2,1)}, bf16[128,128]{1,0:T(8,128)(2,1)})) %all-reduce.3.cloned.1.call-update) | async-done | bytes 65552 | tf_op jit(solution)/shard_map/psum | solution.py:20
  769.2 0.0 copy-start.3
  769.2 1.0 fusion.56
  770.3 0.1 fusion.33
  770.4 0.0 copy-done.2
  770.4 0.7 fusion.25
  771.0 0.0 copy-done.3
  771.1 0.3 fusion.22
  771.3 0.2 fusion.26
  771.6 119.6 %all-gather.3.cloned.1.call-done = bf16[8192,128]{1,0:T(8,128)(2,1)} async-done(((bf16[128,128]{1,0:T(8,128)(2,1)}), bf16[8192,128]{1,0:T(8,128)(2,1)}) %all-gather.3.cloned.1.call-update) | async-done | bytes 2097168 | tf_op jit(solution)/shard_map/all_gather | solution.py:97
  891.2 118.9 %all-gather.5.cloned.1.call-done = bf16[8192,128]{1,0:T(8,128)(2,1)} async-done(((bf16[128,128]{1,0:T(8,128)(2,1)}), bf16[8192,128]{1,0:T(8,128)(2,1)}) %all-gather.5.cloned.1.call-update) | async-done | bytes 2097168 | tf_op jit(solution)/shard_map/all_gather | solution.py:98
  1010.1 3.4 while.19
  1013.6 0.2 copy.18
  1013.8 4.8 convolution_convert_fusion
  1018.6 0.0 reduce-scatter.2.cloned.1.call-update
  1018.7 295.4 %reduce-scatter.2.cloned.1.call-done = bf16[256,512]{1,0:T(8,128)(2,1)} async-done(((bf16[256,4096]{1,0:T(8,128)(2,1)}), bf16[256,512]{1,0:T(8,128)(2,1)}) %reduce-scatter.2.cloned.1.call-update) | async-done | bytes 262160 | tf_op jit(solution)/shard_map/reduce_scatter | solution.py:108
  (133 shorter events, 1.2 us)
Async XLA Ops:
  6.5 8.7 copy-start.1
  6.5 8.7 copy-start
  6.5 762.7 %all-reduce.3.cloned.1.call-start = ((), (), s32[]{:S(2)}) async-start(), calls=%async_computation.4 | async-start | bytes 131072 | tf_op jit(solution)/shard_map/psum | solution.py:20
  8.0 883.2 %all-gather.3.cloned.1.call-start = ((), (), s32[]{:S(2)}) async-start(), calls=%async_computation.1 | async-start | bytes 2129920 | tf_op jit(solution)/shard_map/all_gather | solution.py:97
  11.7 758.6 %copy-start.2 = (bf16[256,128]{1,0:T(8,128)(2,1)S(1)}, bf16[256,128]{1,0:T(8,128)(2,1)}, u32[]{:S(2)}) copy-start(bf16[256,128]{1,0:T(8,128)(2,1)} %param.13) | copy-start | bytes 196612
  13.2 997.0 %all-gather.5.cloned.1.call-start = ((), (), s32[]{:S(2)}) async-start(), calls=%async_computation.2 | async-start | bytes 2129920 | tf_op jit(solution)/shard_map/all_gather | solution.py:98
  13.9 1300.1 %reduce-scatter.2.cloned.1.call-start = ((), (), s32[]{:S(2)}) async-start(), calls=%async_computation.3 | async-start | bytes 2359296 | tf_op jit(solution)/shard_map/reduce_scatter | solution.py:108
  769.2 1.8 copy-start.3
Sparse Core Ops, SparseCore 0:
  10.3 758.8 all-reduce.2
  771.6 119.5 all-gather.2
  893.6 116.4 all-gather.4
  1018.8 295.2 reduce-scatter.1
where the time goes:
time: 1330 us; the launch traced here: 1320 us
  waiting for transfers between devices  1290 us (97%)
  between operations  13.3 us (1%)
    psum x1, waiting for transfers between devices, from_root(): return lax.psum(jnp.where(mine, value, jnp.zeros_like(value)), axis)  754 us
    reduce_scatter x1, waiting for transfers between devices, shards(): lax.psum_scatter(partial_sums.astype(jnp.bfloat16), 'head', scatter_dimen...  295 us
    all_gather x1, waiting for transfers between devices, shards(): lax.all_gather(pass_keys, 'hst', axis=0, tiled=True)  120 us
    all_gather x1, waiting for transfers between devices, shards(): lax.all_gather(pass_values, 'hst', axis=0, tiled=True)  119 us
  transfers between devices with their start and end apart: 4, of which 4 were waited for; matrix products, arithmetic and copies ran while one was open for 1% of the time, Pallas kernels for 0%

commit v1 on v0

v1 whole, which is shorter than its diff:
```python
import math

import jax
import jax.numpy as jnp
from jax import lax
from jax.experimental import pallas as pl
from jax.experimental.pallas import tpu as pltpu
from jax.sharding import PartitionSpec as P

HD = 128
PASS = 128
ANCHOR = 128
GROUPS = 4
ROWS = 256
HALF = ROWS // 2
QROWS = ROWS * GROUPS
HROWS = HALF * GROUPS
SCALE = math.log2(math.e) / math.sqrt(HD)
LOW = -1e30
BF = jnp.bfloat16
F32 = jnp.float32
VM = pl.BlockSpec(memory_space=pltpu.VMEM)
SM = pl.BlockSpec(memory_space=pltpu.SMEM)
ANY = pl.BlockSpec(memory_space=pl.ANY)


def params():
    return pltpu.CompilerParams(vmem_limit_bytes=48 * 1024 * 1024)


def dot_nt(a, b):
    return lax.dot_general(a, b, (((1,), (1,)), ((), ())), preferred_element_type=F32)


def prepare(index_ref, key_ref, value_ref, query_ref, passed_ref, anchor_ref, scaled_ref):
    rows = lax.broadcasted_iota(jnp.int32, (ROWS, PASS), 0)
    pick = jnp.where(rows == index_ref[...], 1.0, 0.0).astype(BF)
    both = jnp.concatenate([key_ref[...], value_ref[...]], axis=1)
    passed_ref[...] = lax.dot_general(
        pick, both, (((0,), (0,)), ((), ())), preferred_element_type=F32
    ).astype(BF)
    anchor_ref[...] = both[:ANCHOR]
    for half in range(2):
        for g in range(GROUPS):
            part = query_ref[half * HALF : (half + 1) * HALF, g * HD : (g + 1) * HD].astype(F32) * SCALE
            high = part.astype(BF)
            low = (part - high.astype(F32)).astype(BF)
            start = half * HROWS + g * HALF
            scaled_ref[start : start + HALF, :] = jnp.concatenate([high, low], axis=1)


def attend(scaled, acc_ref, top_ref, blocks, masks=None, first=False):
    scores = []
    for number, block in enumerate(blocks):
        keys = block[:, :HD]
        s = dot_nt(scaled, jnp.concatenate([keys, keys], axis=1))
        if masks is not None:
            s = jnp.where(masks[number], s, LOW)
        scores.append(s)
    high = None
    for s in scores:
        for j in range(s.shape[1] // HD):
            part = s[:, j * HD : (j + 1) * HD]
            high = part if high is None else jnp.maximum(high, part)
    high = jnp.max(high, axis=1, keepdims=True)
    if first:
        new = jnp.broadcast_to(high, (high.shape[0], HD))
    else:
        old = top_ref[...]
        new = jnp.maximum(old, high)
    total = None
    for s, block in zip(scores, blocks):
        weights = jnp.concatenate(
            [jnp.exp2(s[:, j * HD : (j + 1) * HD] - new).astype(BF) for j in range(s.shape[1] // HD)], axis=1
        )
        values = jnp.concatenate([block[:, HD:], jnp.ones((block.shape[0], HD), BF)], axis=1)
        part = jnp.dot(weights, values, preferred_element_type=F32)
        total = part if total is None else total + part
    if not first:
        shrink = jnp.exp2(old - new)
        total = acc_ref[...] * jnp.concatenate([shrink, shrink], axis=1) + total
    acc_ref[...] = total
    top_ref[...] = new


def own_row(flag_ref, scaled_ref, key_ref, value_ref, near_ref, near2_ref, far_ref, far2_ref, acc_ref, top_ref):
    scaled = scaled_ref[...]
    token = lax.broadcasted_iota(jnp.int32, (QROWS, ROWS), 0)
    token = token % HALF + (token // HROWS) * HALF
    key = lax.broadcasted_iota(jnp.int32, (QROWS, ROWS), 1)
    local = jnp.concatenate([key_ref[...], value_ref[...]], axis=1)
    attend(scaled, acc_ref, top_ref, [local], [key <= token], first=True)

    @pl.when(flag_ref[0] != 0)
    def _():
        attend(scaled_ref[...], acc_ref, top_ref, [near2_ref[:PASS]])

    @pl.when(flag_ref[1] != 0)
    def _():
        attend(scaled_ref[...], acc_ref, top_ref, [near_ref[PASS : 2 * PASS], near2_ref[PASS : 2 * PASS]])

    @pl.when(flag_ref[2] != 0)
    def _():
        attend(scaled_ref[...], acc_ref, top_ref, [near_ref[2 * PASS :], near2_ref[2 * PASS :]])

    @pl.when(flag_ref[3] != 0)
    def _():
        attend(scaled_ref[...], acc_ref, top_ref, [far_ref[...], far2_ref[...]])


def other_rows(flag_ref, scaled_ref, acc_in, top_in, ours_ref, theirs_ref, acc_ref, top_ref):
    acc_ref[...] = acc_in[...]
    top_ref[...] = top_in[...]
    size = 4 * PASS
    for j in range(3):

        @pl.when(flag_ref[4 + j] != 0)
        def _():
            attend(
                scaled_ref[...],
                acc_ref,
                top_ref,
                [ours_ref[j * size : (j + 1) * size], theirs_ref[j * size : (j + 1) * size]],
            )

    @pl.when(flag_ref[7] != 0)
    def _():
        attend(scaled_ref[...], acc_ref, top_ref, [ours_ref[3 * size :]])

    @pl.when(flag_ref[8] != 0)
    def _():
        attend(scaled_ref[...], acc_ref, top_ref, [theirs_ref[3 * size :]])


def finish(half, flag_ref, scaled_ref, acc_in, top_in, ours_ref, theirs_ref, *rest):
    if half == 0:
        weight_ref, attended_ref, *outs, acc_ref, top_ref, held, sem = rest
    else:
        before_ref, weight_ref, *outs, acc_ref, top_ref, held, sem = rest
    copy = pltpu.make_async_copy(weight_ref, held, sem)
    copy.start()
    span = slice(half * HROWS, (half + 1) * HROWS)
    acc_ref[...] = acc_in[span]
    top_ref[...] = top_in[span]
    size = 4 * PASS
    for j in range(3):

        @pl.when(flag_ref[4 + j] != 0)
        def _():
            attend(
                scaled_ref[span],
                acc_ref,
                top_ref,
                [ours_ref[j * size : (j + 1) * size], theirs_ref[j * size : (j + 1) * size]],
            )

    result = (acc_ref[:, :HD] / acc_ref[:, HD:]).astype(BF)
    attended = jnp.concatenate([result[g * HALF : (g + 1) * HALF] for g in range(GROUPS)], axis=1)
    copy.wait()
    x, h = flag_ref[9], flag_ref[10]
    width = GROUPS * HD

    def project(rows, step, side):
        start = pl.multiple_of((lax.rem(x + step, 4) * 2 + side) * width, width)
        return jnp.dot(rows, held[:, pl.ds(start, width)], preferred_element_type=F32).astype(BF)

    for step in range(4):
        outs[step][...] = project(attended, step, 1 - h)
    if half == 0:
        attended_ref[...] = attended
    else:
        whole = jnp.concatenate([before_ref[...], attended], axis=0)
        for step in range(4):
            outs[4 + step][...] = project(whole, step, h)


def shape(*dims, dtype=BF):
    return jax.ShapeDtypeStruct(dims, dtype)


def shards(queries, keys, values, passing_index, out_weight):
    me = lax.axis_index("hst")
    head = lax.axis_index("head")
    y, z, c = me // 16, (me // 2) % 8, me % 2

    def over_z(value, k):
        return lax.ppermute(value, "hst", [(i, i ^ (2 * k)) for i in range(64)])

    def over_core(value):
        return lax.ppermute(value, "hst", [(i, i ^ 1) for i in range(64)])

    def over_y(value, pairs):
        return lax.ppermute(value, "hst", [(16 * a + i, 16 * b + i) for a, b in pairs for i in range(16)])

    flags = jnp.stack(
        [
            c,
            z & 1,
            z & 2,
            z & 4,
            y >= 1,
            y == 3,
            y >= 2,
            (me > 0) & (c == 0),
            c == 1,
            head // 2,
            head % 2,
        ]
    ).astype(jnp.int32)

    passed, anchor, scaled = pl.pallas_call(
        prepare,
        out_shape=(shape(PASS, 2 * HD), shape(ANCHOR, 2 * HD), shape(QROWS, 2 * HD)),
        in_specs=[VM] * 4,
        out_specs=(VM,) * 3,
        compiler_params=params(),
    )(passing_index, keys, values, queries)

    mirror = over_z(passed, 4)
    near = jnp.concatenate([passed] + [over_z(passed, k) for k in (1, 2, 3)], axis=0)
    far = jnp.concatenate([mirror] + [over_z(mirror, k) for k in (1, 2, 3)], axis=0)

    anchor = jnp.where(me == 0, anchor, jnp.zeros_like(anchor))
    sources = [0]
    for bit in (16, 48, 8, 4, 2):
        if bit == 48:
            pairs = [(0, 48), (16, 32)]
        else:
            pairs = [(s, s + bit) for s in sources]
        anchor = anchor + lax.ppermute(anchor, "hst", pairs)
        sources = sources + [b for _, b in pairs]

    rounds = (((0, 1), (1, 2), (2, 3)), ((0, 3),), ((0, 2), (1, 3)))
    near_y = jnp.concatenate([over_y(near, pairs) for pairs in rounds] + [anchor], axis=0)
    far_y = jnp.concatenate([over_y(far, pairs) for pairs in rounds], axis=0)

    near2, far2 = over_core(near), over_core(far)
    near_y2, far_y2 = over_core(near_y), over_core(far_y)

    state = (shape(QROWS, 2 * HD, dtype=F32), shape(QROWS, HD, dtype=F32))
    acc, top = pl.pallas_call(
        own_row,
        out_shape=state,
        in_specs=[SM] + [VM] * 7,
        out_specs=(VM,) * 2,
        compiler_params=params(),
    )(flags, scaled, keys, values, near, near2, far, far2)
    acc, top = pl.pallas_call(
        other_rows,
        out_shape=state,
        in_specs=[SM] + [VM] * 5,
        out_specs=(VM,) * 2,
        compiler_params=params(),
    )(flags, scaled, acc, top, near_y, near_y2)

    width = GROUPS * HD
    scratch = [
        pltpu.VMEM((HROWS, 2 * HD), F32),
        pltpu.VMEM((HROWS, HD), F32),
        pltpu.VMEM(out_weight.shape, BF),
        pltpu.SemaphoreType.DMA,
    ]

    def finish_first(*args):
        finish(0, *args)

    def finish_second(*args):
        finish(1, *args)

    attended, *away_a = pl.pallas_call(
        finish_first,
        out_shape=(shape(HALF, width),) * 5,
        in_specs=[SM] + [VM] * 5 + [ANY],
        out_specs=(VM,) * 5,
        scratch_shapes=scratch,
        compiler_params=params(),
    )(flags, scaled, acc, top, far_y, far_y2, out_weight)
    outs = pl.pallas_call(
        finish_second,
        out_shape=(shape(HALF, width),) * 4 + (shape(ROWS, width),) * 4,
        in_specs=[SM] + [VM] * 6 + [ANY],
        out_specs=(VM,) * 8,
        scratch_shapes=scratch,
        compiler_params=params(),
    )(flags, scaled, acc, top, far_y, far_y2, attended, out_weight)
    away_b, home = outs[:4], outs[4:]

    def sum_over_x(parts):
        total = parts[0].astype(F32)
        for step in (1, 2, 3):
            pairs = [(2 * a + s, 2 * ((a + step) % 4) + s) for a in range(4) for s in range(2)]
            total = total + lax.ppermute(parts[step], "head", pairs).astype(F32)
        return total

    def over_h(value):
        return lax.ppermute(value, "head", [(i, i ^ 1) for i in range(8)])

    other_a = over_h(sum_over_x(away_a).astype(BF))
    other_b = over_h(sum_over_x(away_b).astype(BF))
    mine = sum_over_x(home)
    return (mine + jnp.concatenate([other_a, other_b], axis=0).astype(F32)).astype(BF)


def solution(mesh):
    in_specs = (
        P("hst", "head"),
        P("hst", "head"),
        P("hst", "head"),
        P("hst", None),
        P("head", None),
    )
    out_specs = P("hst", "head")
    return jax.shard_map(shards, mesh=mesh, in_specs=in_specs, out_specs=out_specs, check_vma=False)
```

time: 1330 us -> 167 us (0.13)
  the two profiles are of different devices: /device:TPU:6 before, /device:TPU:249 now
where the time goes in v1:
time: 167 us; the launch traced here: 166 us
  starting transfers between devices  104 us (62%)
  waiting for transfers between devices  28.8 us (17%)
  Pallas kernels  27.1 us (16%)
  local copies, waits for them, and re-layouts  4.33 us (3%)
    ppermute x4, starting transfers between devices, over_core(): return lax.ppermute(value, 'hst', [(i, i ^ 1) for i in range(64)])  30.5 us
    ppermute x9, starting transfers between devices, sum_over_x(): total = total + lax.ppermute(parts[step], 'head', pairs).astype(F32)  29.1 us
    ppermute x2, waiting for transfers between devices, over_h(): return lax.ppermute(value, 'head', [(i, i ^ 1) for i in range(8)])  19.3 us
    ppermute x7, starting transfers between devices, over_z(): return lax.ppermute(value, 'hst', [(i, i ^ 2 * k) for i in range(64)])  19.1 us
    ppermute x2, starting transfers between devices, over_h(): return lax.ppermute(value, 'head', [(i, i ^ 1) for i in range(8)])  14 us
    pallas_call x1, Pallas kernels, shards(): pl.pallas_call(other_rows, out_shape=state, in_specs=[SM] + [VM] * 5, out...  8.99 us
    ppermute x7, waiting for transfers between devices, over_z(): return lax.ppermute(value, 'hst', [(i, i ^ 2 * k) for i in range(64)])  8.36 us
    ppermute x6, starting transfers between devices, over_y(): lax.ppermute(value, 'hst', [(16 * a + i, 16 * b + i) for a, b in pairs fo...  7.74 us
  transfers between devices with their start and end apart: 33, of which 6 were waited for; matrix products, arithmetic and copies ran while one was open for 0% of the time, Pallas kernels for 13%

profile of v1, /device:TPU:249, one launch (start us, length us, event | category | flops | bytes accessed | tf_op | source)
XLA Modules:
  0.0 165.9 jit_solution(13348789055042962140)
XLA Ops:
  0.0 0.9 copy-done
  1.0 0.8 copy-done.1
  1.8 0.8 copy-done.3
  2.6 0.7 copy-done.5
  3.3 0.2 shard_map.55
  3.5 1.9 %collective-permute-start = (bf16[128,256]{1,0:T(8,128)(2,1)S(1)}, bf16[128,256]{1,0:T(8,128)(2,1)S(1)}, u32[]{:S(2)}, u32[]{:S(2)}) collective-permute-start(bf16[128,256]{1,0:T(8,128)(2,1)S(1)} %get-tuple-element.26), channel_id=1, source_target_pairs={{0,16},{8,24},{16,0},{24,8},{32,48},{40,56},{48,32},{56,40},{64,80... | collective-permute-start | bytes 196616 | tf_op jit(solution)/shard_map/ppermute | solution.py:187
  5.4 1.9 %collective-permute-start.1 = (bf16[128,256]{1,0:T(8,128)(2,1)S(1)}, bf16[128,256]{1,0:T(8,128)(2,1)S(1)}, u32[]{:S(2)}, u32[]{:S(2)}) collective-permute-start(bf16[128,256]{1,0:T(8,128)(2,1)S(1)} %get-tuple-element.26), channel_id=1, source_target_pairs={{0,32},{8,40},{16,48},{24,56},{32,0},{40,8},{48,16},{56,24},{64,96... | collective-permute-start | bytes 196616 | tf_op jit(solution)/shard_map/ppermute | solution.py:187
  7.4 5.4 %collective-permute-start.2 = (bf16[128,256]{1,0:T(8,128)(2,1)S(1)}, bf16[128,256]{1,0:T(8,128)(2,1)S(1)}, u32[]{:S(2)}, u32[]{:S(2)}) collective-permute-start(bf16[128,256]{1,0:T(8,128)(2,1)S(1)} %get-tuple-element.26), channel_id=1, source_target_pairs={{0,48},{8,56},{16,32},{24,40},{32,16},{40,24},{48,0},{56,8},{64,11... | collective-permute-start | bytes 196616 | tf_op jit(solution)/shard_map/ppermute | solution.py:187
  12.8 1.9 %collective-permute-start.4 = (bf16[128,256]{1,0:T(8,128)(2,1)S(1)}, bf16[128,256]{1,0:T(8,128)(2,1)S(1)}, u32[]{:S(2)}, u32[]{:S(2)}) collective-permute-start(bf16[128,256]{1,0:T(8,128)(2,1)S(1)} %get-tuple-element.26), channel_id=1, source_target_pairs={{0,64},{8,72},{16,80},{24,88},{32,96},{40,104},{48,112},{56,120},{... | collective-permute-start | bytes 196616 | tf_op jit(solution)/shard_map/ppermute | solution.py:187
  14.8 0.7 collective-permute-start.12
  15.5 0.0 collective-permute-done
  15.5 0.0 collective-permute-done.1
  15.5 1.3 collective-permute-start.10
  16.8 1.3 collective-permute-start.11
  18.1 1.3 collective-permute-start.9
  19.5 0.7 collective-permute-start.13
  20.1 5.5 %collective-permute-done.4 = bf16[128,256]{1,0:T(8,128)(2,1)S(1)} collective-permute-done((bf16[128,256]{1,0:T(8,128)(2,1)S(1)}, bf16[128,256]{1,0:T(8,128)(2,1)S(1)}, u32[]{:S(2)}, u32[]{:S(2)}) %collective-permute-start.4) | collective-permute-done | bytes 65568 | tf_op jit(solution)/shard_map/ppermute | solution.py:187
  25.7 1.9 %collective-permute-start.5 = (bf16[128,256]{1,0:T(8,128)(2,1)S(1)}, bf16[128,256]{1,0:T(8,128)(2,1)S(1)}, u32[]{:S(2)}, u32[]{:S(2)}) collective-permute-start(bf16[128,256]{1,0:T(8,128)(2,1)S(1)} %collective-permute-done.4), channel_id=1, source_target_pairs={{0,16},{8,24},{16,0},{24,8},{32,48},{40,56},{48,32},{56,40},{64,80... | collective-permute-start | bytes 196616 | tf_op jit(solution)/shard_map/ppermute | solution.py:187
  27.6 0.0 collective-permute-done.13
  27.6 1.9 %collective-permute-start.6 = (bf16[128,256]{1,0:T(8,128)(2,1)S(1)}, bf16[128,256]{1,0:T(8,128)(2,1)S(1)}, u32[]{:S(2)}, u32[]{:S(2)}) collective-permute-start(bf16[128,256]{1,0:T(8,128)(2,1)S(1)} %collective-permute-done.4), channel_id=1, source_target_pairs={{0,32},{8,40},{16,48},{24,56},{32,0},{40,8},{48,16},{56,24},{64,96... | collective-permute-start | bytes 196616 | tf_op jit(solution)/shard_map/ppermute | solution.py:187
  29.6 1.4 collective-permute-done.5
  31.0 0.7 collective-permute-start.14
  31.6 0.0 collective-permute-done.14
  31.7 4.1 %collective-permute-start.7 = (bf16[128,256]{1,0:T(8,128)(2,1)S(1)}, bf16[128,256]{1,0:T(8,128)(2,1)S(1)}, u32[]{:S(2)}, u32[]{:S(2)}) collective-permute-start(bf16[128,256]{1,0:T(8,128)(2,1)S(1)} %collective-permute-done.4), channel_id=1, source_target_pairs={{0,48},{8,56},{16,32},{24,40},{32,16},{40,24},{48,0},{56,8},{64,11... | collective-permute-start | bytes 196616 | tf_op jit(solution)/shard_map/ppermute | solution.py:187
  35.8 0.7 collective-permute-start.15
  36.4 0.0 collective-permute-done.15
  36.5 0.7 collective-permute-start.16
  37.2 1.4 collective-permute-done.7
  38.6 1.3 collective-permute-start.18
  39.9 1.3 collective-permute-start.19
  41.2 0.0 copy-start.2
  41.2 0.0 collective-permute-done.10
  41.2 1.3 collective-permute-start.20
  42.5 0.0 collective-permute-done.11
  42.5 0.1 pad_maximum_fusion.ours_ref
  42.6 16.7 %collective-permute-start.17 = (bf16[1664,256]{1,0:T(8,128)(2,1)S(1)}, bf16[1664,256]{1,0:T(8,128)(2,1)}, u32[]{:S(2)}, u32[]{:S(2)}) collective-permute-start(bf16[1664,256]{1,0:T(8,128)(2,1)S(1)} %pad_maximum_fusion.ours_ref), channel_id=1, source_target_pairs={{0,8},{8,0},{16,24},{24,16},{32,40},{40,32},{48,56},{56,48},{64,72... | collective-permute-start | bytes 2555912 | tf_op jit(solution)/shard_map/ppermute | solution.py:190
  59.3 0.0 collective-permute-done.19
  59.4 9.5 %collective-permute-start.21 = (bf16[1536,256]{1,0:T(8,128)(2,1)S(1)}, bf16[1536,256]{1,0:T(8,128)(2,1)S(1)}, u32[]{:S(2)}, u32[]{:S(2)}) collective-permute-start(bf16[1536,256]{1,0:T(8,128)(2,1)S(1)} %constant_dynamic-update-slice_fusion.8.args_4_), channel_id=1, source_target_pairs={{0,8},{8,0},{16,24},{24,16},{32,40},{40,32},{48,56},{56,48},{64,72... | collective-permute-start | bytes 2359304 | tf_op jit(solution)/shard_map/ppermute | solution.py:190
  68.9 1.9 %collective-permute-start.3 = (bf16[512,256]{1,0:T(8,128)(2,1)S(1)}, bf16[512,256]{1,0:T(8,128)(2,1)}, u32[]{:S(2)}, u32[]{:S(2)}) collective-permute-start(bf16[512,256]{1,0:T(8,128)(2,1)S(1)} %constant_dynamic-update-slice_fusion.near_ref), channel_id=1, source_target_pairs={{0,8},{8,0},{16,24},{24,16},{32,40},{40,32},{48,56},{56,48},{64,72... | collective-permute-start | bytes 786440 | tf_op jit(solution)/shard_map/ppermute | solution.py:190
  70.8 2.4 %collective-permute-start.8 = (bf16[512,256]{1,0:T(8,128)(2,1)S(1)}, bf16[512,256]{1,0:T(8,128)(2,1)}, u32[]{:S(2)}, u32[]{:S(2)}) collective-permute-start(bf16[512,256]{1,0:T(8,128)(2,1)S(1)} %constant_dynamic-update-slice_fusion.4.far_ref), channel_id=1, source_target_pairs={{0,8},{8,0},{16,24},{24,16},{32,40},{40,32},{48,56},{56,48},{64,72... | collective-permute-start | bytes 786440 | tf_op jit(solution)/shard_map/ppermute | solution.py:190
  73.3 0.1 stack.67.flag_ref.args_0_
  73.4 0.0 collective-permute-done.3.near2_ref
  73.4 1.1 collective-permute-done.8.far2_ref
  74.5 0.8 copy-done.4
  75.4 7.1 %shard_map.56 = (f32[1024,256]{1,0:T(8,128)S(1)}, f32[1024,128]{1,0:T(8,128)S(1)}) custom-call(s32[11]{0:T(128)S(1)} %stack.67.flag_ref.args_0_, bf16[1024,256]{1,0:T(8,128)(2,1)S(1)} %get-tuple-element.25.scaled_ref.args_1_, bf16[256,128]{1,0:T(8,128)(2,1)S(1)} %copy-done.2, bf16[256,128]{1,0:T(8,128)(2,1)S(1)} %copy-done.4, ...), custom_call_target="tpu_custom_call" | custom-call | tf_op jit(solution)/shard_map/pallas_call | solution.py:241
  82.5 9.0 %shard_map.57 = (f32[1024,256]{1,0:T(8,128)S(1)}, f32[1024,128]{1,0:T(8,128)S(1)}) custom-call(s32[11]{0:T(128)S(1)} %stack.67.flag_ref.args_0_, bf16[1024,256]{1,0:T(8,128)(2,1)S(1)} %get-tuple-element.25.scaled_ref.args_1_, f32[1024,256]{1,0:T(8,128)S(1)} %get-tuple-element.27.acc_in, f32[1024,128]{1,0:T(8,128)S(1)} %get-tuple-element.28.top_in, ...), custom_call_target="tpu_custom_call" | custom-call | tf_op jit(solution)/shard_map/pallas_call | solution.py:248
  91.5 5.1 %shard_map.58 = (bf16[128,512]{1,0:T(8,128)(2,1)S(1)}, bf16[128,512]{1,0:T(8,128)(2,1)S(1)}, bf16[128,512]{1,0:T(8,128)(2,1)S(1)}, bf16[128,512]{1,0:T(8,128)(2,1)S(1)}, bf16[128,512]{1,0:T(8,128)(2,1)S(1)}) custom-call(s32[11]{0:T(128)S(1)} %stack.67.flag_ref.args_0_, bf16[1024,256]{1,0:T(8,128)(2,1)S(1)} %get-tuple-element.25.scaled_ref.args_1_, ...), custom_call_target="tpu_custom_call" | custom-call | tf_op jit(solution)/shard_map/pallas_call | solution.py:270
  96.7 3.1 %collective-permute-start.25 = (bf16[128,512]{1,0:T(8,128)(2,1)S(1)}, bf16[128,512]{1,0:T(8,128)(2,1)S(1)}, u32[]{:S(2)}, u32[]{:S(2)}) collective-permute-start(bf16[128,512]{1,0:T(8,128)(2,1)S(1)} %get-tuple-element.38), channel_id=1, source_target_pairs={{0,2},{1,3},{2,4},{3,5},{4,6},{5,7},{6,0},{7,1},{8,10},{9,11},{10,... | collective-permute-start | bytes 393224 | tf_op jit(solution)/shard_map/ppermute | solution.py:292
  99.8 4.4 %collective-permute-start.26 = (bf16[128,512]{1,0:T(8,128)(2,1)S(1)}, bf16[128,512]{1,0:T(8,128)(2,1)S(1)}, u32[]{:S(2)}, u32[]{:S(2)}) collective-permute-start(bf16[128,512]{1,0:T(8,128)(2,1)S(1)} %get-tuple-element.39), channel_id=1, source_target_pairs={{0,4},{1,5},{2,6},{3,7},{4,0},{5,1},{6,2},{7,3},{8,12},{9,13},{10,... | collective-permute-start | bytes 393224 | tf_op jit(solution)/shard_map/ppermute | solution.py:292
  104.2 3.1 %collective-permute-start.27 = (bf16[128,512]{1,0:T(8,128)(2,1)S(1)}, bf16[128,512]{1,0:T(8,128)(2,1)S(1)}, u32[]{:S(2)}, u32[]{:S(2)}) collective-permute-start(bf16[128,512]{1,0:T(8,128)(2,1)S(1)} %get-tuple-element.40), channel_id=1, source_target_pairs={{0,6},{1,7},{2,0},{3,1},{4,2},{5,3},{6,4},{7,5},{8,14},{9,15},{10,... | collective-permute-start | bytes 393224 | tf_op jit(solution)/shard_map/ppermute | solution.py:292
  107.2 5.7 %shard_map.59 = (bf16[128,512]{1,0:T(8,128)(2,1)S(1)}, bf16[128,512]{1,0:T(8,128)(2,1)S(1)}, bf16[128,512]{1,0:T(8,128)(2,1)S(1)}, bf16[128,512]{1,0:T(8,128)(2,...) custom-call(s32[11]{0:T(128)S(1)} %stack.67.flag_ref.args_0_, ...), custom_call_target="tpu_custom_call" | custom-call | tf_op jit(solution)/shard_map/pallas_call | solution.py:278
  112.9 2.2 %collective-permute-start.29 = (bf16[128,512]{1,0:T(8,128)(2,1)S(1)}, bf16[128,512]{1,0:T(8,128)(2,1)S(1)}, u32[]{:S(2)}, u32[]{:S(2)}) collective-permute-start(bf16[128,512]{1,0:T(8,128)(2,1)S(1)} %get-tuple-element.42), channel_id=1, source_target_pairs={{0,2},{1,3},{2,4},{3,5},{4,6},{5,7},{6,0},{7,1},{8,10},{9,11},{10,... | collective-permute-start | bytes 393224 | tf_op jit(solution)/shard_map/ppermute | solution.py:292
  115.1 2.8 %collective-permute-start.30 = (bf16[128,512]{1,0:T(8,128)(2,1)S(1)}, bf16[128,512]{1,0:T(8,128)(2,1)S(1)}, u32[]{:S(2)}, u32[]{:S(2)}) collective-permute-start(bf16[128,512]{1,0:T(8,128)(2,1)S(1)} %get-tuple-element.43), channel_id=1, source_target_pairs={{0,4},{1,5},{2,6},{3,7},{4,0},{5,1},{6,2},{7,3},{8,12},{9,13},{10,... | collective-permute-start | bytes 393224 | tf_op jit(solution)/shard_map/ppermute | solution.py:292
  118.0 3.4 %collective-permute-start.31 = (bf16[128,512]{1,0:T(8,128)(2,1)S(1)}, bf16[128,512]{1,0:T(8,128)(2,1)S(1)}, u32[]{:S(2)}, u32[]{:S(2)}) collective-permute-start(bf16[128,512]{1,0:T(8,128)(2,1)S(1)} %get-tuple-element.44), channel_id=1, source_target_pairs={{0,6},{1,7},{2,0},{3,1},{4,2},{5,3},{6,4},{7,5},{8,14},{9,15},{10,... | collective-permute-start | bytes 393224 | tf_op jit(solution)/shard_map/ppermute | solution.py:292
  121.4 2.5 %collective-permute-start.22 = (bf16[256,512]{1,0:T(8,128)(2,1)S(1)}, bf16[256,512]{1,0:T(8,128)(2,1)S(1)}, u32[]{:S(2)}, u32[]{:S(2)}) collective-permute-start(bf16[256,512]{1,0:T(8,128)(2,1)S(1)} %get-tuple-element.34), channel_id=1, source_target_pairs={{0,2},{1,3},{2,4},{3,5},{4,6},{5,7},{6,0},{7,1},{8,10},{9,11},{10,... | collective-permute-start | bytes 786440 | tf_op jit(solution)/shard_map/ppermute | solution.py:292
  123.9 3.7 %collective-permute-start.23 = (bf16[256,512]{1,0:T(8,128)(2,1)S(1)}, bf16[256,512]{1,0:T(8,128)(2,1)S(1)}, u32[]{:S(2)}, u32[]{:S(2)}) collective-permute-start(bf16[256,512]{1,0:T(8,128)(2,1)S(1)} %get-tuple-element.35), channel_id=1, source_target_pairs={{0,4},{1,5},{2,6},{3,7},{4,0},{5,1},{6,2},{7,3},{8,12},{9,13},{10,... | collective-permute-start | bytes 786440 | tf_op jit(solution)/shard_map/ppermute | solution.py:292
  127.6 0.1 add_convert_fusion.2
  127.7 4.0 %collective-permute-start.24 = (bf16[256,512]{1,0:T(8,128)(2,1)S(1)}, bf16[256,512]{1,0:T(8,128)(2,1)S(1)}, u32[]{:S(2)}, u32[]{:S(2)}) collective-permute-start(bf16[256,512]{1,0:T(8,128)(2,1)S(1)} %get-tuple-element.36), channel_id=1, source_target_pairs={{0,6},{1,7},{2,0},{3,1},{4,2},{5,3},{6,4},{7,5},{8,14},{9,15},{10,... | collective-permute-start | bytes 786440 | tf_op jit(solution)/shard_map/ppermute | solution.py:292
  131.7 9.5 %collective-permute-start.28 = (bf16[128,512]{1,0:T(8,128)(2,1)S(1)}, bf16[128,512]{1,0:T(8,128)(2,1)S(1)}, u32[]{:S(2)}, u32[]{:S(2)}) collective-permute-start(bf16[128,512]{1,0:T(8,128)(2,1)S(1)} %add_convert_fusion.2), channel_id=1, source_target_pairs={{0,1},{1,0},{2,3},{3,2},{4,5},{5,4},{6,7},{7,6},{8,9},{9,8},{10,11... | collective-permute-start | bytes 393224 | tf_op jit(solution)/shard_map/ppermute | solution.py:296
  141.2 0.1 add_convert_fusion.1
  141.3 4.5 %collective-permute-start.32 = (bf16[128,512]{1,0:T(8,128)(2,1)S(1)}, bf16[128,512]{1,0:T(8,128)(2,1)S(1)}, u32[]{:S(2)}, u32[]{:S(2)}) collective-permute-start(bf16[128,512]{1,0:T(8,128)(2,1)S(1)} %add_convert_fusion.1), channel_id=1, source_target_pairs={{0,1},{1,0},{2,3},{3,2},{4,5},{5,4},{6,7},{7,6},{8,9},{9,8},{10,11... | collective-permute-start | bytes 393224 | tf_op jit(solution)/shard_map/ppermute | solution.py:296
  145.8 16.5 %collective-permute-done.28 = bf16[128,512]{1,0:T(8,128)(2,1)S(1)} collective-permute-done((bf16[128,512]{1,0:T(8,128)(2,1)S(1)}, bf16[128,512]{1,0:T(8,128)(2,1)S(1)}, u32[]{:S(2)}, u32[]{:S(2)}) %collective-permute-start.28) | collective-permute-done | bytes 131104 | tf_op jit(solution)/shard_map/ppermute | solution.py:296
  162.2 2.8 %collective-permute-done.32 = bf16[128,512]{1,0:T(8,128)(2,1)S(1)} collective-permute-done((bf16[128,512]{1,0:T(8,128)(2,1)S(1)}, bf16[128,512]{1,0:T(8,128)(2,1)S(1)}, u32[]{:S(2)}, u32[]{:S(2)}) %collective-permute-start.32) | collective-permute-done | bytes 131104 | tf_op jit(solution)/shard_map/ppermute | solution.py:296
  165.1 0.9 add_convert_fusion
  (41 shorter events, 0.3 us)
Async XLA Ops:
  0.0 0.9 copy-start
  1.0 0.8 copy-start.1
  1.8 0.8 copy-start.3
  2.6 0.7 copy-start.5
  3.5 11.9 %collective-permute-start = (bf16[128,256]{1,0:T(8,128)(2,1)S(1)}, bf16[128,256]{1,0:T(8,128)(2,1)S(1)}, u32[]{:S(2)}, u32[]{:S(2)}) collective-permute-start(bf16[128,256]{1,0:T(8,128)(2,1)S(1)} %get-tuple-element.26), channel_id=1, source_target_pairs={{0,16},{8,24},{16,0},{24,8},{32,48},{40,56},{48,32},{56,40},{64,80... | collective-permute-start | bytes 196616 | tf_op jit(solution)/shard_map/ppermute | solution.py:187
  5.4 10.0 %collective-permute-start.1 = (bf16[128,256]{1,0:T(8,128)(2,1)S(1)}, bf16[128,256]{1,0:T(8,128)(2,1)S(1)}, u32[]{:S(2)}, u32[]{:S(2)}) collective-permute-start(bf16[128,256]{1,0:T(8,128)(2,1)S(1)} %get-tuple-element.26), channel_id=1, source_target_pairs={{0,32},{8,40},{16,48},{24,56},{32,0},{40,8},{48,16},{56,24},{64,96... | collective-permute-start | bytes 196616 | tf_op jit(solution)/shard_map/ppermute | solution.py:187
  7.4 8.1 %collective-permute-start.2 = (bf16[128,256]{1,0:T(8,128)(2,1)S(1)}, bf16[128,256]{1,0:T(8,128)(2,1)S(1)}, u32[]{:S(2)}, u32[]{:S(2)}) collective-permute-start(bf16[128,256]{1,0:T(8,128)(2,1)S(1)} %get-tuple-element.26), channel_id=1, source_target_pairs={{0,48},{8,56},{16,32},{24,40},{32,16},{40,24},{48,0},{56,8},{64,11... | collective-permute-start | bytes 196616 | tf_op jit(solution)/shard_map/ppermute | solution.py:187
  12.8 12.9 %collective-permute-start.4 = (bf16[128,256]{1,0:T(8,128)(2,1)S(1)}, bf16[128,256]{1,0:T(8,128)(2,1)S(1)}, u32[]{:S(2)}, u32[]{:S(2)}) collective-permute-start(bf16[128,256]{1,0:T(8,128)(2,1)S(1)} %get-tuple-element.26), channel_id=1, source_target_pairs={{0,64},{8,72},{16,80},{24,88},{32,96},{40,104},{48,112},{56,120},{... | collective-permute-start | bytes 196616 | tf_op jit(solution)/shard_map/ppermute | solution.py:187
  14.8 4.7 %collective-permute-start.12 = (bf16[128,256]{1,0:T(8,128)(2,1)S(1)}, bf16[128,256]{1,0:T(8,128)(2,1)S(1)}, u32[]{:S(2)}, u32[]{:S(2)}) collective-permute-start(bf16[128,256]{1,0:T(8,128)(2,1)S(1)} %broadcast_select_fusion), channel_id=1, source_target_pairs={{0,128},{1,129},{2,130},{3,131},{4,132},{5,133},{6,134},{7,135}} | collective-permute-start | bytes 196616 | tf_op jit(solution)/shard_map/ppermute | solution.py:230
  15.5 25.7 %collective-permute-start.10 = (bf16[512,256]{1,0:T(8,128)(2,1)S(1)}, bf16[512,256]{1,0:T(8,128)(2,1)S(1)}, u32[]{:S(2)}, u32[]{:S(2)}) collective-permute-start(bf16[512,256]{1,0:T(8,128)(2,1)S(1)} %constant_dynamic-update-slice_fusion.near_ref), channel_id=1, source_target_pairs={{0,384},{8,392},{16,400},{24,408},{32,416},{40,424},{48,432},{56,4... | collective-permute-start | bytes 786440 | tf_op jit(solution)/shard_map/ppermute | solution.py:193
  16.8 25.7 %collective-permute-start.11 = (bf16[512,256]{1,0:T(8,128)(2,1)S(1)}, bf16[512,256]{1,0:T(8,128)(2,1)S(1)}, u32[]{:S(2)}, u32[]{:S(2)}) collective-permute-start(bf16[512,256]{1,0:T(8,128)(2,1)S(1)} %constant_dynamic-update-slice_fusion.near_ref), channel_id=1, source_target_pairs={{0,256},{8,264},{16,272},{24,280},{32,288},{40,296},{48,304},{56,3... | collective-permute-start | bytes 786440 | tf_op jit(solution)/shard_map/ppermute | solution.py:193
  18.1 24.4 %collective-permute-start.9 = (bf16[512,256]{1,0:T(8,128)(2,1)S(1)}, bf16[512,256]{1,0:T(8,128)(2,1)S(1)}, u32[]{:S(2)}, u32[]{:S(2)}) collective-permute-start(bf16[512,256]{1,0:T(8,128)(2,1)S(1)} %constant_dynamic-update-slice_fusion.near_ref), channel_id=1, source_target_pairs={{0,128},{8,136},{16,144},{24,152},{32,160},{40,168},{48,176},{56,1... | collective-permute-start | bytes 786440 | tf_op jit(solution)/shard_map/ppermute | solution.py:193
  19.5 8.1 %collective-permute-start.13 = (bf16[128,256]{1,0:T(8,128)(2,1)S(1)}, bf16[128,256]{1,0:T(8,128)(2,1)S(1)}, u32[]{:S(2)}, u32[]{:S(2)}) collective-permute-start(bf16[128,256]{1,0:T(8,128)(2,1)S(1)} %fusion), channel_id=1, source_target_pairs={{0,384},{128,256},{1,385},{129,257},{2,386},{130,258},{3,387},{131... | collective-permute-start | bytes 196616 | tf_op jit(solution)/shard_map/ppermute | solution.py:230
  25.7 5.3 %collective-permute-start.5 = (bf16[128,256]{1,0:T(8,128)(2,1)S(1)}, bf16[128,256]{1,0:T(8,128)(2,1)S(1)}, u32[]{:S(2)}, u32[]{:S(2)}) collective-permute-start(bf16[128,256]{1,0:T(8,128)(2,1)S(1)} %collective-permute-done.4), channel_id=1, source_target_pairs={{0,16},{8,24},{16,0},{24,8},{32,48},{40,56},{48,32},{56,40},{64,80... | collective-permute-start | bytes 196616 | tf_op jit(solution)/shard_map/ppermute | solution.py:187
  27.6 8.1 %collective-permute-start.6 = (bf16[128,256]{1,0:T(8,128)(2,1)S(1)}, bf16[128,256]{1,0:T(8,128)(2,1)S(1)}, u32[]{:S(2)}, u32[]{:S(2)}) collective-permute-start(bf16[128,256]{1,0:T(8,128)(2,1)S(1)} %collective-permute-done.4), channel_id=1, source_target_pairs={{0,32},{8,40},{16,48},{24,56},{32,0},{40,8},{48,16},{56,24},{64,96... | collective-permute-start | bytes 196616 | tf_op jit(solution)/shard_map/ppermute | solution.py:187
  31.0 0.7 collective-permute-start.14
  31.7 6.9 %collective-permute-start.7 = (bf16[128,256]{1,0:T(8,128)(2,1)S(1)}, bf16[128,256]{1,0:T(8,128)(2,1)S(1)}, u32[]{:S(2)}, u32[]{:S(2)}) collective-permute-start(bf16[128,256]{1,0:T(8,128)(2,1)S(1)} %collective-permute-done.4), channel_id=1, source_target_pairs={{0,48},{8,56},{16,32},{24,40},{32,16},{40,24},{48,0},{56,8},{64,11... | collective-permute-start | bytes 196616 | tf_op jit(solution)/shard_map/ppermute | solution.py:187
  35.8 0.7 collective-permute-start.15
  36.5 3.4 %collective-permute-start.16 = (bf16[128,256]{1,0:T(8,128)(2,1)S(1)}, bf16[128,256]{1,0:T(8,128)(2,1)S(1)}, u32[]{:S(2)}, u32[]{:S(2)}) collective-permute-start(bf16[128,256]{1,0:T(8,128)(2,1)S(1)} %add.64), channel_id=1, source_target_pairs={{0,16},{128,144},{384,400},{256,272},{64,80},{192,208},{448,464},{... | collective-permute-start | bytes 196616 | tf_op jit(solution)/shard_map/ppermute | solution.py:230
  38.6 20.7 %collective-permute-start.18 = (bf16[512,256]{1,0:T(8,128)(2,1)S(1)}, bf16[512,256]{1,0:T(8,128)(2,1)S(1)}, u32[]{:S(2)}, u32[]{:S(2)}) collective-permute-start(bf16[512,256]{1,0:T(8,128)(2,1)S(1)} %constant_dynamic-update-slice_fusion.4.far_ref), channel_id=1, source_target_pairs={{0,128},{8,136},{16,144},{24,152},{32,160},{40,168},{48,176},{56,1... | collective-permute-start | bytes 786440 | tf_op jit(solution)/shard_map/ppermute | solution.py:193
  39.9 19.5 %collective-permute-start.19 = (bf16[512,256]{1,0:T(8,128)(2,1)S(1)}, bf16[512,256]{1,0:T(8,128)(2,1)S(1)}, u32[]{:S(2)}, u32[]{:S(2)}) collective-permute-start(bf16[512,256]{1,0:T(8,128)(2,1)S(1)} %constant_dynamic-update-slice_fusion.4.far_ref), channel_id=1, source_target_pairs={{0,384},{8,392},{16,400},{24,408},{32,416},{40,424},{48,432},{56,4... | collective-permute-start | bytes 786440 | tf_op jit(solution)/shard_map/ppermute | solution.py:193
  41.2 33.3 %copy-start.2 = (bf16[256,128]{1,0:T(8,128)(2,1)S(1)}, bf16[256,128]{1,0:T(8,128)(2,1)}, u32[]{:S(2)}) copy-start(bf16[256,128]{1,0:T(8,128)(2,1)} %key_ref.3) | copy-start | bytes 196612
  41.2 18.2 %collective-permute-start.20 = (bf16[512,256]{1,0:T(8,128)(2,1)S(1)}, bf16[512,256]{1,0:T(8,128)(2,1)S(1)}, u32[]{:S(2)}, u32[]{:S(2)}) collective-permute-start(bf16[512,256]{1,0:T(8,128)(2,1)S(1)} %constant_dynamic-update-slice_fusion.4.far_ref), channel_id=1, source_target_pairs={{0,256},{8,264},{16,272},{24,280},{32,288},{40,296},{48,304},{56,3... | collective-permute-start | bytes 786440 | tf_op jit(solution)/shard_map/ppermute | solution.py:193
  42.6 39.9 %collective-permute-start.17 = (bf16[1664,256]{1,0:T(8,128)(2,1)S(1)}, bf16[1664,256]{1,0:T(8,128)(2,1)}, u32[]{:S(2)}, u32[]{:S(2)}) collective-permute-start(bf16[1664,256]{1,0:T(8,128)(2,1)S(1)} %pad_maximum_fusion.ours_ref), channel_id=1, source_target_pairs={{0,8},{8,0},{16,24},{24,16},{32,40},{40,32},{48,56},{56,48},{64,72... | collective-permute-start | bytes 2555912 | tf_op jit(solution)/shard_map/ppermute | solution.py:190
  59.4 32.1 %collective-permute-start.21 = (bf16[1536,256]{1,0:T(8,128)(2,1)S(1)}, bf16[1536,256]{1,0:T(8,128)(2,1)S(1)}, u32[]{:S(2)}, u32[]{:S(2)}) collective-permute-start(bf16[1536,256]{1,0:T(8,128)(2,1)S(1)} %constant_dynamic-update-slice_fusion.8.args_4_), channel_id=1, source_target_pairs={{0,8},{8,0},{16,24},{24,16},{32,40},{40,32},{48,56},{56,48},{64,72... | collective-permute-start | bytes 2359304 | tf_op jit(solution)/shard_map/ppermute | solution.py:190
  68.9 4.5 %collective-permute-start.3 = (bf16[512,256]{1,0:T(8,128)(2,1)S(1)}, bf16[512,256]{1,0:T(8,128)(2,1)}, u32[]{:S(2)}, u32[]{:S(2)}) collective-permute-start(bf16[512,256]{1,0:T(8,128)(2,1)S(1)} %constant_dynamic-update-slice_fusion.near_ref), channel_id=1, source_target_pairs={{0,8},{8,0},{16,24},{24,16},{32,40},{40,32},{48,56},{56,48},{64,72... | collective-permute-start | bytes 786440 | tf_op jit(solution)/shard_map/ppermute | solution.py:190
  70.8 3.7 %collective-permute-start.8 = (bf16[512,256]{1,0:T(8,128)(2,1)S(1)}, bf16[512,256]{1,0:T(8,128)(2,1)}, u32[]{:S(2)}, u32[]{:S(2)}) collective-permute-start(bf16[512,256]{1,0:T(8,128)(2,1)S(1)} %constant_dynamic-update-slice_fusion.4.far_ref), channel_id=1, source_target_pairs={{0,8},{8,0},{16,24},{24,16},{32,40},{40,32},{48,56},{56,48},{64,72... | collective-permute-start | bytes 786440 | tf_op jit(solution)/shard_map/ppermute | solution.py:190
  74.5 0.8 copy-start.4
  96.7 21.3 %collective-permute-start.25 = (bf16[128,512]{1,0:T(8,128)(2,1)S(1)}, bf16[128,512]{1,0:T(8,128)(2,1)S(1)}, u32[]{:S(2)}, u32[]{:S(2)}) collective-permute-start(bf16[128,512]{1,0:T(8,128)(2,1)S(1)} %get-tuple-element.38), channel_id=1, source_target_pairs={{0,2},{1,3},{2,4},{3,5},{4,6},{5,7},{6,0},{7,1},{8,10},{9,11},{10,... | collective-permute-start | bytes 393224 | tf_op jit(solution)/shard_map/ppermute | solution.py:292
  99.8 21.6 %collective-permute-start.26 = (bf16[128,512]{1,0:T(8,128)(2,1)S(1)}, bf16[128,512]{1,0:T(8,128)(2,1)S(1)}, u32[]{:S(2)}, u32[]{:S(2)}) collective-permute-start(bf16[128,512]{1,0:T(8,128)(2,1)S(1)} %get-tuple-element.39), channel_id=1, source_target_pairs={{0,4},{1,5},{2,6},{3,7},{4,0},{5,1},{6,2},{7,3},{8,12},{9,13},{10,... | collective-permute-start | bytes 393224 | tf_op jit(solution)/shard_map/ppermute | solution.py:292
  104.2 19.7 %collective-permute-start.27 = (bf16[128,512]{1,0:T(8,128)(2,1)S(1)}, bf16[128,512]{1,0:T(8,128)(2,1)S(1)}, u32[]{:S(2)}, u32[]{:S(2)}) collective-permute-start(bf16[128,512]{1,0:T(8,128)(2,1)S(1)} %get-tuple-element.40), channel_id=1, source_target_pairs={{0,6},{1,7},{2,0},{3,1},{4,2},{5,3},{6,4},{7,5},{8,14},{9,15},{10,... | collective-permute-start | bytes 393224 | tf_op jit(solution)/shard_map/ppermute | solution.py:292
  112.9 14.7 %collective-permute-start.29 = (bf16[128,512]{1,0:T(8,128)(2,1)S(1)}, bf16[128,512]{1,0:T(8,128)(2,1)S(1)}, u32[]{:S(2)}, u32[]{:S(2)}) collective-permute-start(bf16[128,512]{1,0:T(8,128)(2,1)S(1)} %get-tuple-element.42), channel_id=1, source_target_pairs={{0,2},{1,3},{2,4},{3,5},{4,6},{5,7},{6,0},{7,1},{8,10},{9,11},{10,... | collective-permute-start | bytes 393224 | tf_op jit(solution)/shard_map/ppermute | solution.py:292
  115.1 16.5 %collective-permute-start.30 = (bf16[128,512]{1,0:T(8,128)(2,1)S(1)}, bf16[128,512]{1,0:T(8,128)(2,1)S(1)}, u32[]{:S(2)}, u32[]{:S(2)}) collective-permute-start(bf16[128,512]{1,0:T(8,128)(2,1)S(1)} %get-tuple-element.43), channel_id=1, source_target_pairs={{0,4},{1,5},{2,6},{3,7},{4,0},{5,1},{6,2},{7,3},{8,12},{9,13},{10,... | collective-permute-start | bytes 393224 | tf_op jit(solution)/shard_map/ppermute | solution.py:292
  118.0 23.2 %collective-permute-start.31 = (bf16[128,512]{1,0:T(8,128)(2,1)S(1)}, bf16[128,512]{1,0:T(8,128)(2,1)S(1)}, u32[]{:S(2)}, u32[]{:S(2)}) collective-permute-start(bf16[128,512]{1,0:T(8,128)(2,1)S(1)} %get-tuple-element.44), channel_id=1, source_target_pairs={{0,6},{1,7},{2,0},{3,1},{4,2},{5,3},{6,4},{7,5},{8,14},{9,15},{10,... | collective-permute-start | bytes 393224 | tf_op jit(solution)/shard_map/ppermute | solution.py:292
  121.4 43.7 %collective-permute-start.22 = (bf16[256,512]{1,0:T(8,128)(2,1)S(1)}, bf16[256,512]{1,0:T(8,128)(2,1)S(1)}, u32[]{:S(2)}, u32[]{:S(2)}) collective-permute-start(bf16[256,512]{1,0:T(8,128)(2,1)S(1)} %get-tuple-element.34), channel_id=1, source_target_pairs={{0,2},{1,3},{2,4},{3,5},{4,6},{5,7},{6,0},{7,1},{8,10},{9,11},{10,... | collective-permute-start | bytes 786440 | tf_op jit(solution)/shard_map/ppermute | solution.py:292
  123.9 41.2 %collective-permute-start.23 = (bf16[256,512]{1,0:T(8,128)(2,1)S(1)}, bf16[256,512]{1,0:T(8,128)(2,1)S(1)}, u32[]{:S(2)}, u32[]{:S(2)}) collective-permute-start(bf16[256,512]{1,0:T(8,128)(2,1)S(1)} %get-tuple-element.35), channel_id=1, source_target_pairs={{0,4},{1,5},{2,6},{3,7},{4,0},{5,1},{6,2},{7,3},{8,12},{9,13},{10,... | collective-permute-start | bytes 786440 | tf_op jit(solution)/shard_map/ppermute | solution.py:292
  127.7 37.4 %collective-permute-start.24 = (bf16[256,512]{1,0:T(8,128)(2,1)S(1)}, bf16[256,512]{1,0:T(8,128)(2,1)S(1)}, u32[]{:S(2)}, u32[]{:S(2)}) collective-permute-start(bf16[256,512]{1,0:T(8,128)(2,1)S(1)} %get-tuple-element.36), channel_id=1, source_target_pairs={{0,6},{1,7},{2,0},{3,1},{4,2},{5,3},{6,4},{7,5},{8,14},{9,15},{10,... | collective-permute-start | bytes 786440 | tf_op jit(solution)/shard_map/ppermute | solution.py:292
  131.7 30.6 %collective-permute-start.28 = (bf16[128,512]{1,0:T(8,128)(2,1)S(1)}, bf16[128,512]{1,0:T(8,128)(2,1)S(1)}, u32[]{:S(2)}, u32[]{:S(2)}) collective-permute-start(bf16[128,512]{1,0:T(8,128)(2,1)S(1)} %add_convert_fusion.2), channel_id=1, source_target_pairs={{0,1},{1,0},{2,3},{3,2},{4,5},{5,4},{6,7},{7,6},{8,9},{9,8},{10,11... | collective-permute-start | bytes 393224 | tf_op jit(solution)/shard_map/ppermute | solution.py:296
  141.3 23.8 %collective-permute-start.32 = (bf16[128,512]{1,0:T(8,128)(2,1)S(1)}, bf16[128,512]{1,0:T(8,128)(2,1)S(1)}, u32[]{:S(2)}, u32[]{:S(2)}) collective-permute-start(bf16[128,512]{1,0:T(8,128)(2,1)S(1)} %add_convert_fusion.1), channel_id=1, source_target_pairs={{0,1},{1,0},{2,3},{3,2},{4,5},{5,4},{6,7},{7,6},{8,9},{9,8},{10,11... | collective-permute-start | bytes 393224 | tf_op jit(solution)/shard_map/ppermute | solution.py:296

commit v2 on v0

v2 whole, which is shorter than its diff:
```python
import math

import jax
import jax.numpy as jnp
from jax import lax
from jax.experimental import pallas as pl
from jax.experimental.pallas import tpu as pltpu
from jax.sharding import PartitionSpec as P

HD = 128
PASS = 128
ANCHOR = 128
GROUPS = 4
ROWS = 256
HALF = ROWS // 2
QROWS = ROWS * GROUPS
HROWS = HALF * GROUPS
TILE = 512
SCALE = math.log2(math.e) / math.sqrt(HD)
LOW = -1e30
BF = jnp.bfloat16
F32 = jnp.float32
VM = pl.BlockSpec(memory_space=pltpu.VMEM)
SM = pl.BlockSpec(memory_space=pltpu.SMEM)
ANY = pl.BlockSpec(memory_space=pl.ANY)


def params():
    return pltpu.CompilerParams(vmem_limit_bytes=20 * 2**20)


def dot_nt(a, b):
    return lax.dot_general(a, b, (((1,), (1,)), ((), ())), preferred_element_type=F32)


def prepare(place_ref, index_ref, key_ref, value_ref, query_ref, passed_ref, anchor_ref, scaled_ref):
    rows = lax.broadcasted_iota(jnp.int32, (ROWS, PASS), 0)
    pick = jnp.where(rows == index_ref[...], 1.0, 0.0).astype(BF)
    both = jnp.concatenate([key_ref[...], value_ref[...]], axis=1)
    passed_ref[...] = lax.dot_general(
        pick, both, (((0,), (0,)), ((), ())), preferred_element_type=F32
    ).astype(BF)
    anchor_ref[...] = jnp.where(place_ref[0] == 0, both[:ANCHOR], jnp.zeros_like(both[:ANCHOR]))
    for half in range(2):
        for g in range(GROUPS):
            part = query_ref[half * HALF : (half + 1) * HALF, g * HD : (g + 1) * HD].astype(F32) * SCALE
            high = part.astype(BF)
            low = (part - high.astype(F32)).astype(BF)
            start = half * HROWS + g * HALF
            scaled_ref[start : start + HALF, :] = jnp.concatenate([high, low], axis=1)


def position(place_ref):
    me = place_ref[0]
    return me // 16, lax.rem(me // 2, 8), lax.rem(me, 2)


def tile(scaled_ref, acc_ref, top_ref, start, key, value, mask, first):
    span = slice(start, start + TILE)
    s = dot_nt(scaled_ref[span], key)
    if mask is not None:
        s = jnp.where(mask, s, LOW)
    parts = [s[:, j * HD : (j + 1) * HD] for j in range(s.shape[1] // HD)]
    high = parts[0]
    for part in parts[1:]:
        high = jnp.maximum(high, part)
    high = jnp.max(high, axis=1, keepdims=True)
    if first:
        new = jnp.broadcast_to(high, (TILE, HD))
    else:
        old = top_ref[span]
        new = jnp.maximum(old, high)
    weights = jnp.concatenate([jnp.exp2(part - new).astype(BF) for part in parts], axis=1)
    total = jnp.dot(weights, value, preferred_element_type=F32)
    if not first:
        shrink = jnp.exp2(old - new)
        total = acc_ref[span] * jnp.concatenate([shrink, shrink], axis=1) + total
    acc_ref[span] = total
    top_ref[span] = new


def attend(scaled_ref, acc_ref, top_ref, blocks, masks=None, first=False):
    block = blocks[0] if len(blocks) == 1 else jnp.concatenate(blocks, axis=0)
    keys, count = block[:, :HD], block.shape[0]
    key = jnp.concatenate([keys, keys], axis=1)
    value = jnp.concatenate([block[:, HD:], jnp.ones((count, HD), BF)], axis=1)
    for number in range(QROWS // TILE):
        mask = None if masks is None else masks[number]
        tile(scaled_ref, acc_ref, top_ref, number * TILE, key, value, mask, first)


def own_tokens(scaled_ref, key_ref, value_ref, acc_ref, top_ref):
    token = lax.broadcasted_iota(jnp.int32, (TILE, ROWS), 0) % HALF
    key = lax.broadcasted_iota(jnp.int32, (TILE, ROWS), 1)
    masks = [key <= token + (number * TILE // HROWS) * HALF for number in range(QROWS // TILE)]
    local = jnp.concatenate([key_ref[...], value_ref[...]], axis=1)
    attend(scaled_ref, acc_ref, top_ref, [local], masks, first=True)


def visit(place_ref, scaled_ref, acc_ref, top_ref, pieces, spots):
    y, z, _ = position(place_ref)
    for row in range(3):

        @pl.when(row < y)
        def _():
            for piece in pieces:
                attend(scaled_ref, acc_ref, top_ref, [piece[row, : 4 * PASS]])

    def own_row(bit):
        parts = []
        for spot, k in enumerate(spots):
            if k and bit <= k < 2 * bit:
                parts += [piece[y, spot * PASS : (spot + 1) * PASS] for piece in pieces]
        return parts

    for bit in (1, 2, 4):
        if any(bit <= k < 2 * bit for k in spots):

            @pl.when(lax.rem(z // bit, 2) == 1)
            def _():
                attend(scaled_ref, acc_ref, top_ref, own_row(bit))


def visit_anchor(place_ref, scaled_ref, acc_ref, top_ref, piece, core):
    me = place_ref[0]

    @pl.when((lax.rem(me, 2) == core) & (me > 0))
    def _():
        attend(scaled_ref, acc_ref, top_ref, [piece[0, 4 * PASS :]])


NEAR = (0, 4, 2, 6)
FAR = (1, 5, 3, 7)


def attend_near(place_ref, scaled_ref, acc_in, top_in, ours_ref, theirs_ref, acc_ref, top_ref):
    acc_ref[...] = acc_in[...]
    top_ref[...] = top_in[...]
    visit(place_ref, scaled_ref, acc_ref, top_ref, [ours_ref, theirs_ref], NEAR)
    y, _, c = position(place_ref)

    @pl.when(c == 1)
    def _():
        attend(scaled_ref, acc_ref, top_ref, [theirs_ref[y, :PASS]])


def attend_far(place_ref, scaled_ref, acc_in, top_in, ours_ref, acc_ref, top_ref):
    acc_ref[...] = acc_in[...]
    top_ref[...] = top_in[...]
    visit(place_ref, scaled_ref, acc_ref, top_ref, [ours_ref], FAR)
    visit_anchor(place_ref, scaled_ref, acc_ref, top_ref, ours_ref, 0)


def finish(place_ref, scaled_ref, acc_in, top_in, theirs_ref, weight_ref, away_ref, home_ref, acc_ref, top_ref, held, sem):
    copy = pltpu.make_async_copy(weight_ref, held, sem)
    copy.start()
    acc_ref[...] = acc_in[...]
    top_ref[...] = top_in[...]
    visit(place_ref, scaled_ref, acc_ref, top_ref, [theirs_ref], FAR)
    visit_anchor(place_ref, scaled_ref, acc_ref, top_ref, theirs_ref, 1)
    result = (acc_ref[:, :HD] / acc_ref[:, HD:]).astype(BF)
    attended = jnp.concatenate(
        [
            jnp.concatenate(
                [result[half * HROWS + g * HALF : half * HROWS + (g + 1) * HALF] for g in range(GROUPS)], axis=1
            )
            for half in range(2)
        ],
        axis=0,
    )
    copy.wait()
    h = lax.rem(place_ref[1], 2)
    width = GROUPS * HD
    for out, side in ((away_ref, 1 - h), (home_ref, h)):
        for x in range(4):
            start = pl.multiple_of((2 * x + side) * width, width)
            out[x] = jnp.dot(attended, held[:, pl.ds(start, width)], preferred_element_type=F32).astype(BF)


def shape(*dims, dtype=BF):
    return jax.ShapeDtypeStruct(dims, dtype)


def shards(queries, keys, values, passing_index, out_weight):
    me = lax.axis_index("hst")
    head = lax.axis_index("head")

    def over_z(value, k):
        return lax.ppermute(value, "hst", [(i, i ^ (2 * k)) for i in range(64)])

    def over_core(value):
        return lax.ppermute(value, "hst", [(i, i ^ 1) for i in range(64)])

    def over_y(value):
        return lax.all_to_all(
            jnp.broadcast_to(value[None], (4,) + value.shape),
            "hst",
            0,
            0,
            axis_index_groups=[[16 * row + i for row in range(4)] for i in range(16)],
        )

    place = jnp.stack([me, head]).astype(jnp.int32)

    def call(kernel, out_shape, specs, *args, flops=0, moved=0, scratch=()):
        many = isinstance(out_shape, tuple)
        return pl.pallas_call(
            kernel,
            out_shape=out_shape,
            in_specs=specs,
            out_specs=(VM,) * len(out_shape) if many else VM,
            scratch_shapes=scratch,
            compiler_params=params(),
            cost_estimate=pl.CostEstimate(flops=flops, bytes_accessed=moved, transcendentals=0),
        )(*args)

    def attention(kernel, *pieces, keys):
        return call(
            kernel,
            state,
            [SM] + [VM] * (3 + len(pieces)),
            place,
            scaled,
            acc,
            top,
            *pieces,
            flops=8 * QROWS * keys * HD,
            moved=2**20,
        )

    state = (shape(QROWS, 2 * HD, dtype=F32), shape(QROWS, HD, dtype=F32))
    passed, anchor, scaled = call(
        prepare,
        (shape(PASS, 2 * HD), shape(ANCHOR, 2 * HD), shape(QROWS, 2 * HD)),
        [SM] + [VM] * 4,
        place,
        passing_index,
        keys,
        values,
        queries,
        moved=2**20,
    )

    def spread(value, k):
        step = 2 * k
        return value + lax.ppermute(value, "hst", [(i, i + step) for i in range(0, 16, 2 * step)])

    acc, top = call(own_tokens, state, [VM] * 3, scaled, keys, values, flops=8 * QROWS * ROWS * HD, moved=2**20)
    mirror, anchor, acc, top = lax.optimization_barrier((over_z(passed, 4), spread(anchor, 4), acc, top))
    two = jnp.concatenate([passed, mirror], axis=0)
    pair, anchor = lax.optimization_barrier((over_z(two, 2), spread(anchor, 2)))
    near = jnp.concatenate([two, pair], axis=0)
    far = jnp.concatenate([over_z(near, 1), spread(anchor, 1)], axis=0)

    near_y, far = lax.optimization_barrier((over_y(near), far))
    far_y = over_y(far)
    acc, top = attention(attend_near, near_y, over_core(near_y), keys=3840)
    far_y, acc, top = lax.optimization_barrier((far_y, acc, top))
    acc, top = attention(attend_far, far_y, keys=2048)
    far_y2 = over_core(far_y)

    width = GROUPS * HD
    away, home = call(
        finish,
        (shape(4, ROWS, width), shape(4, ROWS, width)),
        [SM] + [VM] * 4 + [ANY],
        place,
        scaled,
        acc,
        top,
        far_y2,
        out_weight,
        flops=8 * QROWS * 3072 * HD,
        moved=2**23,
        scratch=[
            pltpu.VMEM((QROWS, 2 * HD), F32),
            pltpu.VMEM((QROWS, HD), F32),
            pltpu.VMEM(out_weight.shape, BF),
            pltpu.SemaphoreType.DMA,
        ],
    )

    def sum_over_x(parts):
        rows = lax.all_to_all(
            parts, "head", 0, 0, axis_index_groups=[[0, 2, 4, 6], [1, 3, 5, 7]], tiled=True
        )
        return jnp.sum(rows.astype(F32), axis=0)

    other = lax.ppermute(sum_over_x(away).astype(BF), "head", [(i, i ^ 1) for i in range(8)])
    return (sum_over_x(home) + other.astype(F32)).astype(BF)


def solution(mesh):
    in_specs = (
        P("hst", "head"),
        P("hst", "head"),
        P("hst", "head"),
        P("hst", None),
        P("head", None),
    )
    out_specs = P("hst", "head")
    return jax.shard_map(shards, mesh=mesh, in_specs=in_specs, out_specs=out_specs, check_vma=False)
```

time: 1330 us -> 153 us (0.12)
  the two profiles are of different devices: /device:TPU:6 before, /device:TPU:187 now
where the time goes in v2:
time: 153 us
  waiting for transfers between devices  48.2 us (32%)
  starting transfers between devices  43.2 us (28%)
  Pallas kernels  25.1 us (16%)
  blocking collectives  17.8 us (12%)
  local copies, waits for them, and re-layouts  16.6 us (11%)
    pallas_call x5, Pallas kernels, call(): pl.pallas_call(kernel, out_shape=out_shape, in_specs=specs, out_specs=(VM...  25.1 us
    ppermute x1, waiting for transfers between devices, shards(): lax.ppermute(sum_over_x(away).astype(BF), 'head', [(i, i ^ 1) for i in ra...  22.8 us
    all_to_all x1, blocking collectives, sum_over_x(): lax.all_to_all(parts, 'head', 0, 0, axis_index_groups=[[0, 2, 4, 6], [1,...  17.8 us
    ppermute x3, waiting for transfers between devices, over_z(): return lax.ppermute(value, 'hst', [(i, i ^ 2 * k) for i in range(64)])  15.1 us
    unnamed x38, local copies, waits for them, and re-layouts  14.4 us
    ppermute x3, starting transfers between devices, over_z(): return lax.ppermute(value, 'hst', [(i, i ^ 2 * k) for i in range(64)])  11 us
    all_to_all x2, starting transfers between devices, over_y(): lax.all_to_all(jnp.broadcast_to(value[None], (4,) + value.shape), 'hst',...  10.1 us
    ppermute x1, starting transfers between devices, shards(): lax.ppermute(sum_over_x(away).astype(BF), 'head', [(i, i ^ 1) for i in ra...  9.28 us
  transfers between devices with their start and end apart: 12, of which 7 were waited for; matrix products, arithmetic and copies ran while one was open for 1% of the time, Pallas kernels for 10%

profile of v2, /device:TPU:187, one launch (start us, length us, event | category | flops | bytes accessed | tf_op | source)
XLA Modules:
  0.0 152.5 jit_solution(1799306813641603880)
XLA Ops:
  0.0 0.1 pad_add_fusion.place_ref
  0.1 0.0 copy-start
  0.1 0.9 copy-done
  1.0 0.0 copy-start.1
  1.0 0.8 copy-done.1
  1.9 0.0 copy-start.3
  1.9 0.8 copy-done.3
  2.7 0.0 copy-start.5
  2.7 0.7 copy-done.5
  3.4 0.8 shard_map.55
  4.1 0.0 copy-start.7
  4.1 0.7 collective-permute-start.1
  4.8 1.9 %collective-permute-start = (bf16[128,256]{1,0:T(8,128)(2,1)S(1)}, bf16[128,256]{1,0:T(8,128)(2,1)S(1)}, u32[]{:S(2)}, u32[]{:S(2)}) collective-permute-start(bf16[128,256]{1,0:T(8,128)(2,1)S(1)} %get-tuple-element.28), channel_id=1, source_target_pairs={{0,64},{8,72},{16,80},{24,88},{32,96},{40,104},{48,112},{56,120},{... | collective-permute-start | bytes 196616 | tf_op jit(solution)/shard_map/ppermute | solution.py:189
  6.7 0.0 copy-start.2
  6.8 0.8 copy-done.2
  7.6 0.0 copy-start.4
  7.6 0.8 copy-done.4
  8.4 0.9 shard_map.56
  9.3 0.0 copy-start.10
  9.3 1.0 copy-done.10
  10.3 0.0 collective-permute-done.1
  10.3 4.9 %collective-permute-done = bf16[128,256]{1,0:T(8,128)(2,1)S(1)} collective-permute-done((bf16[128,256]{1,0:T(8,128)(2,1)S(1)}, bf16[128,256]{1,0:T(8,128)(2,1)S(1)}, u32[]{:S(2)}, u32[]{:S(2)}) %collective-permute-start) | collective-permute-done | bytes 65568 | tf_op jit(solution)/shard_map/ppermute | solution.py:189
  15.2 7.1 %collective-permute-start.2 = (bf16[256,256]{1,0:T(8,128)(2,1)S(1)}, bf16[256,256]{1,0:T(8,128)(2,1)S(1)}, u32[]{:S(2)}, u32[]{:S(2)}) collective-permute-start(bf16[256,256]{1,0:T(8,128)(2,1)S(1)} %pad_maximum_fusion.1), channel_id=1, source_target_pairs={{0,32},{8,40},{16,48},{24,56},{32,0},{40,8},{48,16},{56,24},{64,96... | collective-permute-start | bytes 393224 | tf_op jit(solution)/shard_map/ppermute | solution.py:189
  22.4 0.0 copy-done.7
  22.4 0.7 collective-permute-start.3
  23.1 0.0 copy-done.12
  23.1 0.0 collective-permute-done.3
  23.2 3.9 %collective-permute-done.2 = bf16[256,256]{1,0:T(8,128)(2,1)S(1)} collective-permute-done((bf16[256,256]{1,0:T(8,128)(2,1)S(1)}, bf16[256,256]{1,0:T(8,128)(2,1)S(1)}, u32[]{:S(2)}, u32[]{:S(2)}) %collective-permute-start.2) | collective-permute-done | bytes 131104 | tf_op jit(solution)/shard_map/ppermute | solution.py:189
  27.1 1.0 broadcast_in_dim.4
  28.1 4.8 %all-to-all-start = ((bf16[4,512,256]{2,1,0:T(8,128)(2,1)}), bf16[4,512,256]{2,1,0:T(8,128)(2,1)S(1)}, u32[]{:S(2)}, u32[]{:S(2)}) async-start(bf16[4,512,256]{2,1,0:T(8,128)(2,1)} %broadcast_in_dim.4), calls=%async_computation | async-start | bytes 2097152 | tf_op jit(solution)/shard_map/all_to_all | solution.py:195
  32.9 1.9 %collective-permute-start.4 = (bf16[512,256]{1,0:T(8,128)(2,1)S(1)}, bf16[512,256]{1,0:T(8,128)(2,1)S(1)}, u32[]{:S(2)}, u32[]{:S(2)}) collective-permute-start(bf16[512,256]{1,0:T(8,128)(2,1)S(1)} %constant_dynamic-update-slice_fusion), channel_id=1, source_target_pairs={{0,16},{8,24},{16,0},{24,8},{32,48},{40,56},{48,32},{56,40},{64,80... | collective-permute-start | bytes 786440 | tf_op jit(solution)/shard_map/ppermute | solution.py:189
  34.9 0.7 collective-permute-start.5
  35.5 0.0 collective-permute-done.5
  35.6 6.3 %collective-permute-done.4 = bf16[512,256]{1,0:T(8,128)(2,1)S(1)} collective-permute-done((bf16[512,256]{1,0:T(8,128)(2,1)S(1)}, bf16[512,256]{1,0:T(8,128)(2,1)S(1)}, u32[]{:S(2)}, u32[]{:S(2)}) %collective-permute-start.4) | collective-permute-done | bytes 262176 | tf_op jit(solution)/shard_map/ppermute | solution.py:189
  41.9 3.9 %all-to-all-done.ours_ref = bf16[4,512,256]{2,1,0:T(8,128)(2,1)S(1)} async-done(((bf16[4,512,256]{2,1,0:T(8,128)(2,1)}), bf16[4,512,256]{2,1,0:T(8,128)(2,1)S(1)}, u32[]{:S(2)}, u32[]{:S(2)}) %all-to-all-start) | async-done | bytes 1048608 | tf_op jit(solution)/shard_map/all_to_all | solution.py:195
  45.9 3.2 %collective-permute-start.6 = (bf16[4,512,256]{2,1,0:T(8,128)(2,1)S(1)}, bf16[4,512,256]{2,1,0:T(8,128)(2,1)S(1)}, u32[]{:S(2)}, u32[]{:S(2)}) collective-permute-start(bf16[4,512,256]{2,1,0:T(8,128)(2,1)S(1)} %all-to-all-done.ours_ref), channel_id=1, source_target_pairs={{0,8},{8,0},{16,24},{24,16},{32,40},{40,32},{48,56},{56,48},{64,72... | collective-permute-start | bytes 3145736 | tf_op jit(solution)/shard_map/ppermute | solution.py:192
  49.1 1.2 broadcast_in_dim.5
  50.3 5.3 %all-to-all-start.1 = ((bf16[4,640,256]{2,1,0:T(8,128)(2,1)}), bf16[4,640,256]{2,1,0:T(8,128)(2,1)S(1)}, u32[]{:S(2)}, u32[]{:S(2)}) async-start(bf16[4,640,256]{2,1,0:T(8,128)(2,1)} %broadcast_in_dim.5), calls=%async_computation.1 | async-start | bytes 2621440 | tf_op jit(solution)/shard_map/all_to_all | solution.py:195
  55.6 0.0 collective-permute-done.6.theirs_ref
  55.6 1.0 copy-done.8
  56.6 1.2 copy-done.11
  57.9 1.0 copy-done.13
  58.9 8.2 %shard_map.57 = (f32[1024,256]{1,0:T(8,128)S(1)}, f32[1024,128]{1,0:T(8,128)S(1)}) custom-call(s32[2]{0:T(128)S(1)} %pad_add_fusion.place_ref, bf16[1024,256]{1,0:T(8,128)(2,1)S(1)} %copy-done.8, f32[1024,256]{1,0:T(8,128)S(1)} %copy-done.11, f32[1024,128]{1,0:T(8,128)S(1)} %copy-done.13, bf16[4,512,256]{2,1,0:T(8,128)(2,1)S(1)} %all-to-all-done.ours_ref, ...), custom_call_target="tpu_custom_call" | custom-call | flops 4026531840 | bytes 1048576 | tf_op jit(solution)/shard_map/pallas_call | solution.py:207
  67.1 0.0 copy-start.14
  67.1 1.0 copy-done.14
  68.1 0.8 copy-done.16
  68.9 3.0 %all-to-all-done.1.ours_ref = bf16[4,640,256]{2,1,0:T(8,128)(2,1)S(1)} async-done(((bf16[4,640,256]{2,1,0:T(8,128)(2,1)}), bf16[4,640,256]{2,1,0:T(8,128)(2,1)S(1)}, u32[]{:S(2)}, u32[]{:S(2)}) %all-to-all-start.1) | async-done | bytes 1310752 | tf_op jit(solution)/shard_map/all_to_all | solution.py:195
  71.9 3.0 %collective-permute-start.7 = (bf16[4,640,256]{2,1,0:T(8,128)(2,1)S(1)}, bf16[4,640,256]{2,1,0:T(8,128)(2,1)S(1)}, u32[]{:S(2)}, u32[]{:S(2)}) collective-permute-start(bf16[4,640,256]{2,1,0:T(8,128)(2,1)S(1)} %all-to-all-done.1.ours_ref), channel_id=1, source_target_pairs={{0,8},{8,0},{16,24},{24,16},{32,40},{40,32},{48,56},{56,48},{64,72... | collective-permute-start | bytes 3932168 | tf_op jit(solution)/shard_map/ppermute | solution.py:192
  74.8 0.0 copy-start.9
  74.8 1.0 copy-done.9
  75.9 1.2 copy-done.15
  77.1 1.0 copy-done.17
  78.1 6.1 %shard_map.58 = (f32[1024,256]{1,0:T(8,128)S(1)}, f32[1024,128]{1,0:T(8,128)S(1)}) custom-call(s32[2]{0:T(128)S(1)} %pad_add_fusion.place_ref, bf16[1024,256]{1,0:T(8,128)(2,1)S(1)} %copy-done.9, f32[1024,256]{1,0:T(8,128)S(1)} %copy-done.15, f32[1024,128]{1,0:T(8,128)S(1)} %copy-done.17, bf16[4,640,256]{2,1,0:T(8,128)(2,1)S(1)} %all-to-all-done.1.ours_ref), custom_call_target="tpu_custom_call" | custom-call | flops 2147483648 | bytes 1048576 | tf_op jit(solution)/shard_map/pallas_call | solution.py:207
  84.2 0.0 collective-permute-done.7.theirs_ref
  84.2 0.0 copy-done.6
  84.2 9.2 %shard_map.59 = (bf16[4,256,512]{2,1,0:T(8,128)(2,1)S(1)}, bf16[4,256,512]{2,1,0:T(8,128)(2,1)}) custom-call(s32[2]{0:T(128)S(1)} %pad_add_fusion.place_ref, bf16[1024,256]{1,0:T(8,128)(2,1)S(1)} %copy-done.9, f32[1024,256]{1,0:T(8,128)S(1)} %get-tuple-element.45.acc_in, f32[1024,128]{1,0:T(8,128)S(1)} %get-tuple-element.46.top_in, ...), custom_call_target="tpu_custom_call" | custom-call | flops 3221225472 | bytes 8388608 | tf_op jit(solution)/shard_map/pallas_call | solution.py:207
  93.4 17.8 %all_to_all.20 = bf16[4,256,512]{2,1,0:T(8,128)(2,1)S(1)} all-to-all(bf16[4,256,512]{2,1,0:T(8,128)(2,1)S(1)} %get-tuple-element.48), channel_id=1, replica_groups={{0,2,4,6},{1,3,5,7},{8,10,12,14},{9,11,13,15},{16,18,20,22},{17,19,21,2..., dimensions={0} | all-to-all | bytes 2097152 | tf_op jit(solution)/shard_map/all_to_all | solution.py:284
  111.2 4.7 %all-to-all-start.2 = ((bf16[4,256,512]{2,1,0:T(8,128)(2,1)}), bf16[4,256,512]{2,1,0:T(8,128)(2,1)S(1)}, u32[]{:S(2)}, u32[]{:S(2)}) async-start(bf16[4,256,512]{2,1,0:T(8,128)(2,1)} %get-tuple-element.47), calls=%async_computation.2 | async-start | bytes 2097152 | tf_op jit(solution)/shard_map/all_to_all | solution.py:284
  115.9 0.2 reduce_sum.22
  116.1 9.3 %collective-permute-start.8 = (bf16[256,512]{1,0:T(8,128)(2,1)S(1)}, bf16[256,512]{1,0:T(8,128)(2,1)S(1)}, u32[]{:S(2)}, u32[]{:S(2)}) collective-permute-start(bf16[256,512]{1,0:T(8,128)(2,1)S(1)} %reduce_sum.22), channel_id=1, source_target_pairs={{0,1},{1,0},{2,3},{3,2},{4,5},{5,4},{6,7},{7,6},{8,9},{9,8},{10,11... | collective-permute-start | bytes 786440 | tf_op jit(solution)/shard_map/ppermute | solution.py:289
  125.4 3.3 %all-to-all-done.2 = bf16[4,256,512]{2,1,0:T(8,128)(2,1)S(1)} async-done(((bf16[4,256,512]{2,1,0:T(8,128)(2,1)}), bf16[4,256,512]{2,1,0:T(8,128)(2,1)S(1)}, u32[]{:S(2)}, u32[]{:S(2)}) %all-to-all-start.2) | async-done | bytes 1048608 | tf_op jit(solution)/shard_map/all_to_all | solution.py:284
  128.8 0.2 convert_reduce_fusion
  128.9 22.8 %collective-permute-done.8 = bf16[256,512]{1,0:T(8,128)(2,1)S(1)} collective-permute-done((bf16[256,512]{1,0:T(8,128)(2,1)S(1)}, bf16[256,512]{1,0:T(8,128)(2,1)S(1)}, u32[]{:S(2)}, u32[]{:S(2)}) %collective-permute-start.8) | collective-permute-done | bytes 262176 | tf_op jit(solution)/shard_map/ppermute | solution.py:289
  151.7 0.8 add_convert_fusion
  (16 shorter events, 0.1 us)
Async XLA Ops:
  0.1 0.9 copy-start
  1.0 0.8 copy-start.1
  1.9 0.8 copy-start.3
  2.7 0.7 copy-start.5
  4.1 18.3 %copy-start.7 = (bf16[1024,256]{1,0:T(8,128)(2,1)}, bf16[1024,256]{1,0:T(8,128)(2,1)S(1)}, u32[]{:S(2)}) copy-start(bf16[1024,256]{1,0:T(8,128)(2,1)S(1)} %get-tuple-element.27.scaled_ref) | copy-start | bytes 1572868
  4.1 6.2 %collective-permute-start.1 = (bf16[128,256]{1,0:T(8,128)(2,1)S(1)}, bf16[128,256]{1,0:T(8,128)(2,1)S(1)}, u32[]{:S(2)}, u32[]{:S(2)}) collective-permute-start(bf16[128,256]{1,0:T(8,128)(2,1)S(1)} %get-tuple-element.29), channel_id=1, source_target_pairs={{0,64},{1,65},{2,66},{3,67},{4,68},{5,69},{6,70},{7,71}} | collective-permute-start | bytes 196616 | tf_op jit(solution)/shard_map/ppermute | solution.py:246
  4.8 10.4 %collective-permute-start = (bf16[128,256]{1,0:T(8,128)(2,1)S(1)}, bf16[128,256]{1,0:T(8,128)(2,1)S(1)}, u32[]{:S(2)}, u32[]{:S(2)}) collective-permute-start(bf16[128,256]{1,0:T(8,128)(2,1)S(1)} %get-tuple-element.28), channel_id=1, source_target_pairs={{0,64},{8,72},{16,80},{24,88},{32,96},{40,104},{48,112},{56,120},{... | collective-permute-start | bytes 196616 | tf_op jit(solution)/shard_map/ppermute | solution.py:189
  6.7 0.8 copy-start.2
  7.6 0.8 copy-start.4
  9.3 1.0 copy-start.10
  10.3 12.8 %copy-start.12 = (f32[1024,128]{1,0:T(8,128)}, f32[1024,128]{1,0:T(8,128)S(1)}, u32[]{:S(2)}) copy-start(f32[1024,128]{1,0:T(8,128)S(1)} %get-tuple-element.38.top_in) | copy-start | bytes 1572868
  15.2 11.8 %collective-permute-start.2 = (bf16[256,256]{1,0:T(8,128)(2,1)S(1)}, bf16[256,256]{1,0:T(8,128)(2,1)S(1)}, u32[]{:S(2)}, u32[]{:S(2)}) collective-permute-start(bf16[256,256]{1,0:T(8,128)(2,1)S(1)} %pad_maximum_fusion.1), channel_id=1, source_target_pairs={{0,32},{8,40},{16,48},{24,56},{32,0},{40,8},{48,16},{56,24},{64,96... | collective-permute-start | bytes 393224 | tf_op jit(solution)/shard_map/ppermute | solution.py:189
  22.4 0.7 collective-permute-start.3
  28.1 17.8 %all-to-all-start = ((bf16[4,512,256]{2,1,0:T(8,128)(2,1)}), bf16[4,512,256]{2,1,0:T(8,128)(2,1)S(1)}, u32[]{:S(2)}, u32[]{:S(2)}) async-start(bf16[4,512,256]{2,1,0:T(8,128)(2,1)} %broadcast_in_dim.4), calls=%async_computation | async-start | bytes 2097152 | tf_op jit(solution)/shard_map/all_to_all | solution.py:195
  32.9 9.0 %collective-permute-start.4 = (bf16[512,256]{1,0:T(8,128)(2,1)S(1)}, bf16[512,256]{1,0:T(8,128)(2,1)S(1)}, u32[]{:S(2)}, u32[]{:S(2)}) collective-permute-start(bf16[512,256]{1,0:T(8,128)(2,1)S(1)} %constant_dynamic-update-slice_fusion), channel_id=1, source_target_pairs={{0,16},{8,24},{16,0},{24,8},{32,48},{40,56},{48,32},{56,40},{64,80... | collective-permute-start | bytes 786440 | tf_op jit(solution)/shard_map/ppermute | solution.py:189
  34.9 0.7 collective-permute-start.5
  45.9 9.7 %collective-permute-start.6 = (bf16[4,512,256]{2,1,0:T(8,128)(2,1)S(1)}, bf16[4,512,256]{2,1,0:T(8,128)(2,1)S(1)}, u32[]{:S(2)}, u32[]{:S(2)}) collective-permute-start(bf16[4,512,256]{2,1,0:T(8,128)(2,1)S(1)} %all-to-all-done.ours_ref), channel_id=1, source_target_pairs={{0,8},{8,0},{16,24},{24,16},{32,40},{40,32},{48,56},{56,48},{64,72... | collective-permute-start | bytes 3145736 | tf_op jit(solution)/shard_map/ppermute | solution.py:192
  50.3 21.6 %all-to-all-start.1 = ((bf16[4,640,256]{2,1,0:T(8,128)(2,1)}), bf16[4,640,256]{2,1,0:T(8,128)(2,1)S(1)}, u32[]{:S(2)}, u32[]{:S(2)}) async-start(bf16[4,640,256]{2,1,0:T(8,128)(2,1)} %broadcast_in_dim.5), calls=%async_computation.1 | async-start | bytes 2621440 | tf_op jit(solution)/shard_map/all_to_all | solution.py:195
  55.6 1.0 copy-start.8
  56.6 1.2 copy-start.11
  57.9 1.0 copy-start.13
  67.1 1.0 copy-start.14
  68.1 0.8 copy-start.16
  71.9 12.4 %copy-start.6 = (bf16[512,4096]{1,0:T(8,128)(2,1)S(1)}, bf16[512,4096]{1,0:T(8,128)(2,1)}, u32[]{:S(2)}) copy-start(bf16[512,4096]{1,0:T(8,128)(2,1)} %weight_ref.1) | copy-start | bytes 12582916
  71.9 12.3 %collective-permute-start.7 = (bf16[4,640,256]{2,1,0:T(8,128)(2,1)S(1)}, bf16[4,640,256]{2,1,0:T(8,128)(2,1)S(1)}, u32[]{:S(2)}, u32[]{:S(2)}) collective-permute-start(bf16[4,640,256]{2,1,0:T(8,128)(2,1)S(1)} %all-to-all-done.1.ours_ref), channel_id=1, source_target_pairs={{0,8},{8,0},{16,24},{24,16},{32,40},{40,32},{48,56},{56,48},{64,72... | collective-permute-start | bytes 3932168 | tf_op jit(solution)/shard_map/ppermute | solution.py:192
  74.8 1.0 copy-start.9
  75.9 1.2 copy-start.15
  77.1 1.0 copy-start.17
  111.2 17.5 %all-to-all-start.2 = ((bf16[4,256,512]{2,1,0:T(8,128)(2,1)}), bf16[4,256,512]{2,1,0:T(8,128)(2,1)S(1)}, u32[]{:S(2)}, u32[]{:S(2)}) async-start(bf16[4,256,512]{2,1,0:T(8,128)(2,1)} %get-tuple-element.47), calls=%async_computation.2 | async-start | bytes 2097152 | tf_op jit(solution)/shard_map/all_to_all | solution.py:284
  116.1 35.6 %collective-permute-start.8 = (bf16[256,512]{1,0:T(8,128)(2,1)S(1)}, bf16[256,512]{1,0:T(8,128)(2,1)S(1)}, u32[]{:S(2)}, u32[]{:S(2)}) collective-permute-start(bf16[256,512]{1,0:T(8,128)(2,1)S(1)} %reduce_sum.22), channel_id=1, source_target_pairs={{0,1},{1,0},{2,3},{3,2},{4,5},{5,4},{6,7},{7,6},{8,9},{9,8},{10,11... | collective-permute-start | bytes 786440 | tf_op jit(solution)/shard_map/ppermute | solution.py:289
